TPU v7x, 32 devices: a whole 2x2x4 slice. The times are simulated.
32 devices in a mesh: region: 8 (over z, x), member: 4 (over y, core).
Axes of the slice: x: 2, y: 2, z: 4, core: 2. Of those that a mesh axis runs over, the one named last changes fastest.
Arguments:
- ensemble: bfloat16 [128, 16, 64, 512], P('region', 'member'), may hold values from -6 to 6
- increment: bfloat16 [128, 64, 512], P('region'), may hold values from -6 to 6
- coords: bfloat16 [128, 2, 512], P('region'), may hold values from -4.5 to 5.5
- sent_slots: int32 [8, 8, 1], P('region'), may hold values from 0 to 15, as said below
- pair_list: int32 [128, 2], P('region'), may hold values from 0 to 7, as said below
- pair_count: int32 [8], P('region'), may hold values from 8 to 16, as said below
Outputs:
- covariance_product: float32 [128, 64, 512], P('region', 'member')
Inputs may be any that keep to these rules, and one draw needn't show every extreme that they name: `sent_slots`: the k numbers of one home and owner are distinct. `pair_list`: the two slots of a row differ; every received slot is named by some live row of its owner. `pair_count`: some owner has exactly 16 live pairs and some has 8.
All inputs are finite; a program needn't handle non-finite values.
Results may differ from a plain program's by a relative error of at most 0.0028.
Values may be sent and summed in bfloat16 or wider, within the bound.
A program may use at most 128 MiB of HBM per device.

v0:
```python
import jax
import jax.numpy as jnp
from jax import lax
from jax.sharding import PartitionSpec as P

PAIR_GROUP = 4


def gaspari_cohn(distance):
    inside_part = (
        ((-0.25 * distance + 0.5) * distance + 0.625) * distance - 5.0 / 3.0
    ) * distance * distance + 1.0
    floored = jnp.maximum(distance, 1.0)
    outside_part = (
        ((((distance / 12.0 - 0.5) * distance + 0.625) * distance + 5.0 / 3.0) * distance - 5.0)
        * distance
        + 4.0
        - 2.0 / (3.0 * floored)
    )
    return jnp.where(distance <= 1.0, inside_part, jnp.where(distance < 2.0, outside_part, 0.0))


def tile_of(left_where, right_where):
    left_float = left_where.astype(jnp.float32)
    right_float = right_where.astype(jnp.float32)
    east_gap = left_float[0][:, None] - right_float[0][None, :]
    north_gap = left_float[1][:, None] - right_float[1][None, :]
    return gaspari_cohn(jnp.sqrt(east_gap * east_gap + north_gap * north_gap)).astype(jnp.bfloat16)


def pair_terms(member_rows, places, pair_rows_all, live_total):
    slot_total, row_total, points = member_rows.shape
    start_totals = jnp.zeros((slot_total, row_total, points), jnp.float32)
    turn_count = (live_total + PAIR_GROUP - 1) // PAIR_GROUP
    tile_batch = jax.vmap(tile_of)

    def one_turn(turn_index, totals):
        pair_rows = lax.dynamic_slice_in_dim(pair_rows_all, turn_index * PAIR_GROUP, PAIR_GROUP, 0)
        first_slot = pair_rows[:, 0]
        second_slot = pair_rows[:, 1]
        live_flags = (
            turn_index * PAIR_GROUP + jnp.arange(PAIR_GROUP, dtype=jnp.int32) < live_total
        ).astype(jnp.float32)
        tiles = tile_batch(
            jnp.take(places, first_slot, axis=0), jnp.take(places, second_slot, axis=0)
        )
        rows_first = jnp.take(member_rows, first_slot, axis=0)
        rows_second = jnp.take(member_rows, second_slot, axis=0)
        to_first = jnp.einsum(
            "gjq,gpq->gjp", rows_second, tiles, preferred_element_type=jnp.float32
        )
        to_second = jnp.einsum(
            "gjp,gpq->gjq", rows_first, tiles, preferred_element_type=jnp.float32
        )
        for within in range(PAIR_GROUP):
            totals = totals.at[first_slot[within]].add(live_flags[within] * to_first[within])
            totals = totals.at[second_slot[within]].add(live_flags[within] * to_second[within])
        return totals

    return lax.fori_loop(0, turn_count, one_turn, start_totals)


def per_device(ensemble, increment, coords, sent_slots, pair_list, pair_count):
    blocks, members, levels, points = ensemble.shape
    regions = lax.axis_size("region")
    per_home = sent_slots.shape[2]
    slot_total = regions * per_home
    all_members = members * lax.axis_size("member")
    weighted = (ensemble.astype(jnp.float32) * increment[:, None].astype(jnp.float32)).astype(
        jnp.bfloat16
    )
    flat_blocks = weighted.reshape(blocks, members * levels, points)

    def diag_one(pair_entry):
        member_rows, places = pair_entry
        local_tile = tile_of(places, places)
        return lax.dot_general(
            member_rows, local_tile, (((1,), (1,)), ((), ())), preferred_element_type=jnp.float32
        )

    diagonal = lax.map(diag_one, (flat_blocks, coords))
    flat_slots = sent_slots[0].reshape(slot_total)
    places_out = jnp.take(coords, flat_slots, axis=0).reshape(regions, per_home, 2, points)
    live_total = pair_count[0]
    outgoing = jnp.take(weighted, flat_slots, axis=0).reshape(
        regions, per_home, members, levels, points
    )
    got_weighted, got_places = (
        lax.all_to_all(outgoing, "region", split_axis=0, concat_axis=0, tiled=True),
        lax.all_to_all(places_out, "region", split_axis=0, concat_axis=0, tiled=True),
    )
    member_rows = got_weighted.reshape(slot_total, members * levels, points)
    places = got_places.reshape(slot_total, 2, points)
    totals = pair_terms(member_rows, places, pair_list, live_total)
    returned = lax.all_to_all(
        totals.reshape(regions, per_home, members, levels, points),
        "region",
        split_axis=0,
        concat_axis=0,
        tiled=True,
    )
    gathered_back = (
        jnp.zeros((blocks, members, levels, points), jnp.float32)
        .at[flat_slots]
        .add(returned.reshape(slot_total, members, levels, points))
    )
    combined = diagonal.reshape(blocks, members, levels, points) + gathered_back
    member_part = jnp.sum(ensemble.astype(jnp.float32) * combined, axis=1)
    summed = lax.psum_scatter(member_part, "member", scatter_dimension=1, tiled=True)
    return summed / (all_members - 1)


def solution(mesh):
    in_specs = (
        P("region", "member", None, None),
        P("region", None, None),
        P("region", None, None),
        P("region", None, None),
        P("region", None),
        P("region"),
    )
    out_specs = P("region", "member", None)
    return jax.shard_map(
        per_device, mesh=mesh, in_specs=in_specs, out_specs=out_specs, check_vma=False
    )
```

profile of v0, /device:TPU:1, one launch (start us, length us, event | category | flops | bytes accessed | tf_op | source)
XLA Modules:
  0.0 490.7 jit_solution(4858988996713758570)
XLA Ops:
  9.9 6.4 %all-to-all-start.1 = ((bf16[8,1,2,512]{3,2,1,0:T(2,128)(2,1)}), bf16[8,1,2,512]{3,2,1,0:T(2,128)(2,1)S(1)}, u32[]{:S(2)}, u32[]{:S(2)}) async-start(bf16[8,1,2,512]{3,2,1,0:T(2,128)(2,1)} %broadcast_select_fusion.2), calls=%async_computation.1 | async-start | bytes 32768 | tf_op jit(solution)/shard_map/all_to_all | solution.py:90
  17.8 5.4 %fusion.93 = bf16[16,4,64,512]{3,2,1,0:T(8,128)(2,1)} fusion(bf16[16,4,64,512]{3,2,1,0:T(8,128)(2,1)} %param.30, f32[16,64,512]{2,1,0:T(8,128)S(1)} %convert_element_type.50), kind=kLoop, calls=%fused_computation.159 | loop fusion | flops 6291456 | bytes 10485760 | tf_op jit(solution)/shard_map/convert_element_type | solution.py:69
  27.7 5.6 %all-to-all-start = ((bf16[8,1,4,64,512]{4,3,2,1,0:T(8,128)(2,1)}), bf16[8,1,4,64,512]{4,3,2,1,0:T(8,128)(2,1)S(1)}, u32[]{:S(2)}, u32[]{:S(2)}) async-start(bf16[8,1,4,64,512]{4,3,2,1,0:T(8,128)(2,1)} %fusion.95), calls=%async_computation | async-start | bytes 4194304 | tf_op jit(solution)/shard_map/all_to_all | solution.py:89
  34.0 46.1 %all-to-all-done = bf16[8,1,4,64,512]{4,3,2,1,0:T(8,128)(2,1)S(1)} async-done(((bf16[8,1,4,64,512]{4,3,2,1,0:T(8,128)(2,1)}), bf16[8,1,4,64,512]{4,3,2,1,0:T(8,128)(2,1)S(1)}, u32[]{:S(2)}, u32[]{:S(2)}) %all-to-all-start) | async-done | bytes 2097184 | tf_op jit(solution)/shard_map/all_to_all | solution.py:89
  82.5 126.4 %while.33 = (s32[]{:T(128)}, f32[8,256,512]{2,1,0:T(8,128)}, s32[]{:T(128)}, s32[16,2]{0,1:T(2,128)S(1)}, s32[]{:T(128)}, /*index=5*/bf16[8,256,512]{2,1,0:T(8,1...) while((s32[]{:T(128)}, f32[8,256,512]{2,1,0:T(8,128)}, ...), condition=%wide.region_11.14_spmd, body=%wide.region_2.13_spmd.sunk | while | flops 1147160832 | bytes 40145856 | solution.py:60
  87.0 7.4 %fusion.137 = f32[4,256,512]{2,1,0:T(8,128)} fusion(f32[4,512]{1,0:T(4,128)S(1)} %bitcast.129, f32[4,512]{1,0:T(4,128)S(1)} %bitcast.131, f32[4,512]{1,0:T(4,128)S(1)} %bitcast.133, f32[4,512]{1,0:T(4,128)S(1)} %bitcast.135, bf16[4,256,512]{2,1,0:T(8,128)(2,1)S(1)} %gather_fusion.2, pred[4]{0:T(512)(128)(4,1)S(1)} %get-tuple-element.421), kind=kOutput, calls=%fused_computation.58.clone.1 | convolution fusion | flops 571998208 | bytes 3178500 | tf_op jit(solution)/shard_map/while/body/gjq,gpq->gjp/dot_general | solution.py:49
  102.3 3.4 fusion.139
  106.4 6.7 %fusion.140 = f32[4,256,512]{2,1,0:T(8,128)S(1)} fusion(f32[4,512]{1,0:T(4,128)S(1)} %bitcast.130, f32[4,512]{1,0:T(4,128)S(1)} %bitcast.132, f32[4,512]{1,0:T(4,128)S(1)} %bitcast.134, f32[4,512]{1,0:T(4,128)S(1)} %bitcast.136, bf16[4,256,512]{2,1,0:T(8,128)(2,1)S(1)} %gather_fusion.3, pred[4]{0:T(512)(128)(4,1)S(1)} %get-tuple-element.419), kind=kOutput, calls=%fused_computation.57.clone.1 | convolution fusion | flops 571998208 | bytes 3178500 | tf_op jit(solution)/shard_map/while/body/gjp,gpq->gjq/dot_general | solution.py:52
  132.6 3.5 fusion.144
  150.2 7.4 %fusion.137 = f32[4,256,512]{2,1,0:T(8,128)} fusion(f32[4,512]{1,0:T(4,128)S(1)} %bitcast.129, f32[4,512]{1,0:T(4,128)S(1)} %bitcast.131, f32[4,512]{1,0:T(4,128)S(1)} %bitcast.133, f32[4,512]{1,0:T(4,128)S(1)} %bitcast.135, bf16[4,256,512]{2,1,0:T(8,128)(2,1)S(1)} %gather_fusion.2, pred[4]{0:T(512)(128)(4,1)S(1)} %get-tuple-element.421), kind=kOutput, calls=%fused_computation.58.clone.1 | convolution fusion | flops 571998208 | bytes 3178500 | tf_op jit(solution)/shard_map/while/body/gjq,gpq->gjp/dot_general | solution.py:49
  165.5 3.5 fusion.139
  169.6 6.7 %fusion.140 = f32[4,256,512]{2,1,0:T(8,128)S(1)} fusion(f32[4,512]{1,0:T(4,128)S(1)} %bitcast.130, f32[4,512]{1,0:T(4,128)S(1)} %bitcast.132, f32[4,512]{1,0:T(4,128)S(1)} %bitcast.134, f32[4,512]{1,0:T(4,128)S(1)} %bitcast.136, bf16[4,256,512]{2,1,0:T(8,128)(2,1)S(1)} %gather_fusion.3, pred[4]{0:T(512)(128)(4,1)S(1)} %get-tuple-element.419), kind=kOutput, calls=%fused_computation.57.clone.1 | convolution fusion | flops 571998208 | bytes 3178500 | tf_op jit(solution)/shard_map/while/body/gjp,gpq->gjq/dot_general | solution.py:52
  195.9 3.5 fusion.144
  208.9 131.7 %all-to-all-start.2 = ((f32[8,1,4,64,512]{4,3,2,1,0:T(8,128)}), f32[8,1,4,64,512]{4,3,2,1,0:T(8,128)}, u32[]{:S(2)}, u32[]{:S(2)}) async-start(f32[8,1,4,64,512]{4,3,2,1,0:T(8,128)} %bitcast.37), calls=%async_computation.2 | async-start | bytes 8388608 | tf_op jit(solution)/shard_map/all_to_all | solution.py:95
  340.9 65.5 %while.32 = (s32[]{:T(128)}, f32[16,256,512]{2,1,0:T(8,128)}, bf16[16,256,512]{2,1,0:T(8,128)(2,1)}, bf16[16,2,512]{2,1,0:T(2,128)(2,1)}, s32[]{:T(128)}) while((s32[]{:T(128)}, f32[16,256,512]{2,1,0:T(8,128)}, bf16[16,256,512]{2,1,0:T(8,128)(2,1)}, bf16[16,2,512]{2,1,0:T(2,128)(2,1)}, s32[]{:T(128)}) %tuple.134), condition=%wide.region_1.2_spmd, body=%wide.region_0.1_spmd.sunk | while | flops 142869504 | bytes 810057 | solution.py:81
  345.7 3.4 fusion.128
  349.8 3.4 fusion.128
  353.9 3.4 fusion.128
  358.0 3.4 fusion.128
  362.1 3.4 fusion.128
  370.2 3.4 fusion.128
  374.3 3.4 fusion.128
  378.4 3.4 fusion.128
  382.5 3.4 fusion.128
  386.6 3.4 fusion.128
  390.7 3.4 fusion.128
  394.8 3.4 fusion.128
  403.0 3.4 fusion.128
  406.4 26.9 %all-to-all-done.2 = f32[8,1,4,64,512]{4,3,2,1,0:T(8,128)} async-done(((f32[8,1,4,64,512]{4,3,2,1,0:T(8,128)}), f32[8,1,4,64,512]{4,3,2,1,0:T(8,128)}, u32[]{:S(2)}, u32[]{:S(2)}) %all-to-all-start.2) | async-done | bytes 4194336 | tf_op jit(solution)/shard_map/all_to_all | solution.py:95
  433.3 9.0 %scatter_fusion = f32[16,4,64,512]{3,2,1,0:T(8,128)} fusion(f32[16,4,64,512]{3,2,1,0:T(8,128)} %bitcast.126, s32[8]{0:T(128)S(1)} %copy-done.5, f32[8,4,64,512]{3,2,1,0:T(8,128)} %bitcast.38), kind=kCustom, calls=%fused_computation.6 | custom fusion | flops 1048576 | bytes 12582944 | tf_op jit(solution)/shard_map/scatter-add | solution.py:105
  442.3 7.7 %fusion.94 = f32[16,64,512]{2,1,0:T(8,128)} fusion(f32[16,4,64,512]{3,2,1,0:T(8,128)} %scatter_fusion, bf16[16,4,64,512]{3,2,1,0:T(8,128)(2,1)} %param.30), kind=kLoop, calls=%fused_computation.160 | loop fusion | flops 5767168 | bytes 14680064 | tf_op jit(solution)/shard_map/reduce_sum | solution.py:108
  450.0 31.9 %reduce-scatter.2.cloned.1.call-done = f32[16,16,512]{2,1,0:T(8,128)} async-done(((f32[16,64,512]{2,1,0:T(8,128)}), f32[16,16,512]{2,1,0:T(8,128)}) %reduce-scatter.2.cloned.1.call-update) | async-done | bytes 524304 | tf_op jit(solution)/shard_map/reduce_scatter | solution.py:109
  (117 shorter events, 89.3 us)
Async XLA Ops:
  7.2 0.7 copy-start.4
  9.9 17.8 %all-to-all-start.1 = ((bf16[8,1,2,512]{3,2,1,0:T(2,128)(2,1)}), bf16[8,1,2,512]{3,2,1,0:T(2,128)(2,1)S(1)}, u32[]{:S(2)}, u32[]{:S(2)}) async-start(bf16[8,1,2,512]{3,2,1,0:T(2,128)(2,1)} %broadcast_select_fusion.2), calls=%async_computation.1 | async-start | bytes 32768 | tf_op jit(solution)/shard_map/all_to_all | solution.py:90
  27.7 54.8 %copy-start.2 = (s32[3]{0:T(128)S(1)}, s32[3]{0:T(128)}, u32[]{:S(2)}) copy-start(s32[3]{0:T(128)} %constant.410.clone.1) | copy-start | bytes 40
  27.7 54.8 %copy-start.3 = (s32[16,2]{0,1:T(2,128)S(1)}, s32[16,2]{0,1:T(2,128)}, u32[]{:S(2)}) copy-start(s32[16,2]{0,1:T(2,128)} %param.34) | copy-start | bytes 388
  27.7 52.4 %all-to-all-start = ((bf16[8,1,4,64,512]{4,3,2,1,0:T(8,128)(2,1)}), bf16[8,1,4,64,512]{4,3,2,1,0:T(8,128)(2,1)S(1)}, u32[]{:S(2)}, u32[]{:S(2)}) async-start(bf16[8,1,4,64,512]{4,3,2,1,0:T(8,128)(2,1)} %fusion.95), calls=%async_computation | async-start | bytes 4194304 | tf_op jit(solution)/shard_map/all_to_all | solution.py:89
  113.1 1.3 copy-start
  125.2 10.9 %copy-start.1 = (f32[4,256,512]{2,1,0:T(8,128)S(1)}, f32[4,256,512]{2,1,0:T(8,128)}, u32[]{:S(2)}) copy-start(f32[4,256,512]{2,1,0:T(8,128)} %copy-done) | copy-start | bytes 6291460 | tf_op jit(solution)/shard_map/while
  176.3 1.3 copy-start
  188.4 10.9 %copy-start.1 = (f32[4,256,512]{2,1,0:T(8,128)S(1)}, f32[4,256,512]{2,1,0:T(8,128)}, u32[]{:S(2)}) copy-start(f32[4,256,512]{2,1,0:T(8,128)} %copy-done) | copy-start | bytes 6291460 | tf_op jit(solution)/shard_map/while
  208.9 224.3 %all-to-all-start.2 = ((f32[8,1,4,64,512]{4,3,2,1,0:T(8,128)}), f32[8,1,4,64,512]{4,3,2,1,0:T(8,128)}, u32[]{:S(2)}, u32[]{:S(2)}) async-start(f32[8,1,4,64,512]{4,3,2,1,0:T(8,128)} %bitcast.37), calls=%async_computation.2 | async-start | bytes 8388608 | tf_op jit(solution)/shard_map/all_to_all | solution.py:95
  340.6 141.3 %reduce-scatter.2.cloned.1.call-start = ((), (), s32[]{:S(2)}) async-start(), calls=%async_computation.4 | async-start | bytes 2621440 | tf_op jit(solution)/shard_map/reduce_scatter | solution.py:109
  340.9 92.4 %copy-start.5 = (s32[8]{0:T(128)S(1)}, s32[8]{0:T(128)}, u32[]{:S(2)}) copy-start(s32[8]{0:T(128)} %copy-done.4) | copy-start | bytes 100
Sparse Core Ops, SparseCore 0:
  450.2 31.7 reduce-scatter.1
where the time goes:
time: 495 us; the launch traced here: 491 us
  starting transfers between devices  144 us (29%)
  waiting for transfers between devices  105 us (21%)
  other arithmetic  97.8 us (20%)
  matrix products  82.6 us (17%)
  loops' own time  30.2 us (6%)
  local copies, waits for them, and re-layouts  17.2 us (3%)
  between operations  14.1 us (3%)
    all_to_all x1, starting transfers between devices, per_device(): lax.all_to_all(totals.reshape(regions, per_home, members, levels, points)...  132 us
    dot_general x16, matrix products, diag_one(): lax.dot_general(member_rows, local_tile, (((1,), (1,)), ((), ())), prefer...  54.4 us
    all_to_all x1, waiting for transfers between devices, per_device(): lax.all_to_all(outgoing, 'region', split_axis=0, concat_axis=0, tiled=True)  46.1 us
    reduce_scatter x1, waiting for transfers between devices, per_device(): lax.psum_scatter(member_part, 'member', scatter_dimension=1, tiled=True)  31.9 us
    another operation x1, loops' own time, pair_terms(): return lax.fori_loop(0, turn_count, one_turn, start_totals)  30.2 us
    all_to_all x1, waiting for transfers between devices, per_device(): lax.all_to_all(totals.reshape(regions, per_home, members, levels, points)...  26.9 us
    scatter-add x8, other arithmetic, one_turn(): totals.at[first_slot[within]].add(live_flags[within] * to_first[within])  26.8 us
    scatter-add x8, other arithmetic, one_turn(): totals.at[second_slot[within]].add(live_flags[within] * to_second[within])  26 us
  transfers between devices with their start and end apart: 4, of which 3 were waited for; matrix products, arithmetic and copies ran while one was open for 16% of the time, Pallas kernels for 0%

commit v1 on v0

v1 whole, which is shorter than its diff:
```python
import functools

import jax
import jax.numpy as jnp
from jax import lax
from jax.experimental import pallas as pl
from jax.experimental.pallas import tpu as pltpu
from jax.sharding import PartitionSpec as P

MESH = pl.DeviceIdType.MESH
ROWS = 32
TILE_BYTES = 24 << 20


def left_right(where):
    east, north = where[0:1], where[1:2]
    norm = east * east + north * north
    high = norm.astype(jnp.bfloat16).astype(jnp.float32)
    middle = (norm - high).astype(jnp.bfloat16).astype(jnp.float32)
    low = norm - high - middle
    row = lax.broadcasted_iota(jnp.int32, (16, where.shape[1]), 0)

    def stack(entries):
        out = jnp.zeros(row.shape, jnp.float32)
        for k, entry in enumerate(entries):
            out = jnp.where(row == k, entry, out)
        return out.astype(jnp.bfloat16)

    return (
        stack([east, north, high, middle, low, 1.0, 1.0, 1.0]),
        stack([-2.0 * east, -2.0 * north, 1.0, 1.0, 1.0, high, middle, low]),
    )


def gaspari_cohn(square):
    square = jnp.maximum(square, 2.0**-10)
    inverse = lax.rsqrt(square)
    z = square * inverse
    far = jnp.maximum(2.0 - z, 0.0)
    near = jnp.maximum(1.0 - z, 0.0)
    far = far * far
    near = near * near
    near = near + near
    both = square + z
    total = (far * far) * (both + (z - 0.5)) + (near * near) * (2.0 - both)
    return (total * (inverse * (1.0 / 12.0))).astype(jnp.bfloat16)


def kernel(
    regions, groups, levels,
    slots_ref, many_ref, ens_ref, inc_ref, where_ref,
    out_ref,
    place_out, place_in, rows_out, rows_in, weights, field, tiles, square, diag_part, diag_in,
    pair_part, pair_in, home_out, home_in,
    place_send, place_recv, rows_send, rows_recv, diag_send, diag_recv, pair_send, pair_recv,
    home_send, home_recv,
):
    blocks, rows, points = ens_ref.shape
    members = rows // levels
    share = levels // groups
    me = lax.axis_index("region")
    my_group = lax.axis_index("member")

    def to_region(src, dst, send, recv, d):
        return pltpu.make_async_remote_copy(
            src_ref=src.at[d], dst_ref=dst.at[d], send_sem=send.at[d], recv_sem=recv.at[d],
            device_id=(lax.rem(me + d, regions), my_group), device_id_type=MESH,
        )

    def back_to_region(src, dst, send, recv, d):
        return pltpu.make_async_remote_copy(
            src_ref=src.at[d], dst_ref=dst.at[d], send_sem=send.at[d], recv_sem=recv.at[d],
            device_id=(lax.rem(me + regions - d, regions), my_group), device_id_type=MESH,
        )

    def to_group(src, dst, send, recv, d):
        other = lax.rem(my_group + d, groups)
        return pltpu.make_async_remote_copy(
            src_ref=src.at[other], dst_ref=dst.at[d], send_sem=send.at[d], recv_sem=recv.at[d],
            device_id=(me, other), device_id_type=MESH,
        )

    barrier = pltpu.get_barrier_semaphore()

    @pl.loop(1, regions)
    def _(d):
        pl.semaphore_signal(
            barrier, inc=1, device_id=(lax.rem(me + d, regions), my_group), device_id_type=MESH
        )

    @pl.loop(1, groups)
    def _(d):
        pl.semaphore_signal(
            barrier, inc=1, device_id=(me, lax.rem(my_group + d, groups)), device_id_type=MESH
        )

    for d in range(regions):
        slot = slots_ref[lax.rem(me + d, regions)]
        places, sent = (place_in, rows_in) if d == 0 else (place_out, rows_out)
        places[d] = where_ref[slot]
        sent[d, 0:rows] = ens_ref[slot]
        sent[d, rows : rows + levels] = inc_ref[slot]
    pl.semaphore_wait(barrier, regions + groups - 2)

    @pl.loop(1, regions)
    def _(d):
        to_region(place_out, place_in, place_send, place_recv, d).start()

    @pl.loop(1, regions)
    def _(d):
        to_region(rows_out, rows_in, rows_send, rows_recv, d).start()

    def weigh(member_rows, factor):
        factor = factor.astype(jnp.float32)
        return jnp.concatenate(
            [
                (member_rows[m * levels : (m + 1) * levels].astype(jnp.float32) * factor).astype(
                    jnp.bfloat16
                )
                for m in range(members)
            ],
            0,
        )

    def over_members(member_rows, results):
        total = None
        for m in range(members):
            cut = slice(m * levels, (m + 1) * levels)
            term = member_rows[cut].astype(jnp.float32) * results[cut]
            total = term if total is None else total + term
        return total

    def make_tile(index, left_where, right_where):
        left, _ = left_right(left_where)
        _, right = left_right(right_where)
        square[...] = lax.dot_general(
            left, right, (((0,), (0,)), ((), ())), preferred_element_type=jnp.float32
        )

        @pl.loop(0, points // ROWS)
        def _(step):
            cut = pl.ds(pl.multiple_of(step * ROWS, ROWS), ROWS)
            tiles[index, cut] = gaspari_cohn(square[cut])

    @pl.loop(0, blocks)
    def _(b):
        make_tile(0, where_ref[b], where_ref[b])
        member_rows = ens_ref[b]
        results = jnp.dot(
            weigh(member_rows, inc_ref[b]), tiles[0], preferred_element_type=jnp.float32
        )
        total = over_members(member_rows, results)
        for g in range(groups):
            diag_part[g, b] = total[g * share : (g + 1) * share]

    @pl.loop(1, groups)
    def _(d):
        to_group(diag_part, diag_in, diag_send, diag_recv, d).start()

    @pl.loop(1, regions)
    def _(d):
        to_region(place_out, place_in, place_send, place_recv, d).wait()

    keep = tiles.shape[0] > 1
    if keep:

        @pl.loop(1, regions)
        def _(v):
            @pl.loop(0, v)
            def _(u):
                make_tile(v * (v - 1) // 2 + u, place_in[u], place_in[v])

    field[...] = jnp.zeros_like(field)
    weights[0] = weigh(rows_in[0, 0:rows], rows_in[0, rows : rows + levels])

    @pl.loop(1, regions)
    def _(v):
        to_region(rows_out, rows_in, rows_send, rows_recv, v).wait()
        weights[v] = weigh(rows_in[v, 0:rows], rows_in[v, rows : rows + levels])
        second = lax.rem(me + regions - v, regions)

        @pl.loop(0, v)
        def _(u):
            first = lax.rem(me + regions - u, regions)
            times = many_ref[first * regions + second]
            index = v * (v - 1) // 2 + u if keep else 0
            if not keep:
                make_tile(0, place_in[u], place_in[v])
            field[u] += times * lax.dot_general(
                weights[v], tiles[index], (((1,), (1,)), ((), ())),
                preferred_element_type=jnp.float32,
            )
            field[v] += times * jnp.dot(
                weights[u], tiles[index], preferred_element_type=jnp.float32
            )

    @pl.loop(0, regions)
    def _(d):
        total = over_members(rows_in[d, 0:rows], field[d]).astype(pair_part.dtype)
        for g in range(groups):
            pair_part[g, d] = total[g * share : (g + 1) * share]

    @pl.loop(1, groups)
    def _(d):
        to_group(pair_part, pair_in, pair_send, pair_recv, d).start()

    @pl.loop(1, groups)
    def _(d):
        to_group(diag_part, diag_in, diag_send, diag_recv, d).wait()

    @pl.loop(1, groups)
    def _(d):
        to_group(pair_part, pair_in, pair_send, pair_recv, d).wait()

    for d in range(regions):
        total = pair_part[my_group, d].astype(jnp.float32)
        for g in range(1, groups):
            total = total + pair_in[g, d].astype(jnp.float32)
        (home_in if d == 0 else home_out)[d] = total

    @pl.loop(1, regions)
    def _(d):
        back_to_region(home_out, home_in, home_send, home_recv, d).start()

    @pl.loop(0, blocks)
    def _(b):
        total = diag_part[my_group, b]
        for g in range(1, groups):
            total = total + diag_in[g, b]
        out_ref[b] = total

    @pl.loop(1, regions)
    def _(d):
        back_to_region(home_out, home_in, home_send, home_recv, d).wait()

    @pl.loop(0, blocks)
    def _(b):
        total = out_ref[b]
        for d in range(regions):
            here = jnp.where(slots_ref[lax.rem(me + d, regions)] == b, 1.0, 0.0)
            total = total + here * home_in[d]
        out_ref[b] = total


def per_device(ensemble, increment, coords, sent_slots, pair_list, pair_count):
    blocks, members, levels, points = ensemble.shape
    regions, groups = lax.axis_size("region"), lax.axis_size("member")
    share = levels // groups
    rows = members * levels
    live = jnp.arange(pair_list.shape[0], dtype=jnp.int32) < pair_count[0]
    low = jnp.min(pair_list, axis=1)
    high = jnp.max(pair_list, axis=1)
    home = jnp.arange(regions, dtype=jnp.int32)
    first, second = home[:, None, None], home[None, :, None]
    hit = (jnp.minimum(first, second) == low) & (jnp.maximum(first, second) == high) & live
    many = jnp.sum(hit.astype(jnp.float32), axis=2).reshape(regions * regions)
    where = jnp.pad(coords.astype(jnp.float32), ((0, 0), (0, 6), (0, 0)))
    pairs = regions * (regions - 1) // 2
    tile_total = pairs if pairs * points * points * 2 <= TILE_BYTES else 1
    part_kind = jnp.bfloat16 if share % 16 == 0 else jnp.float32
    vmem, smem = pl.BlockSpec(memory_space=pltpu.VMEM), pl.BlockSpec(memory_space=pltpu.SMEM)
    region_dma = pltpu.SemaphoreType.DMA((regions,))
    group_dma = pltpu.SemaphoreType.DMA((groups,))
    f32, bf16 = jnp.float32, jnp.bfloat16
    summed = pl.pallas_call(
        functools.partial(kernel, regions, groups, levels),
        out_shape=jax.ShapeDtypeStruct((blocks, share, points), f32),
        in_specs=[smem, smem, vmem, vmem, vmem],
        out_specs=vmem,
        scratch_shapes=[
            pltpu.VMEM((regions, 8, points), f32),
            pltpu.VMEM((regions, 8, points), f32),
            pltpu.VMEM((regions, rows + levels, points), bf16),
            pltpu.VMEM((regions, rows + levels, points), bf16),
            pltpu.VMEM((regions, rows, points), bf16),
            pltpu.VMEM((regions, rows, points), f32),
            pltpu.VMEM((tile_total, points, points), bf16),
            pltpu.VMEM((points, points), f32),
            pltpu.VMEM((groups, blocks, share, points), f32),
            pltpu.VMEM((groups, blocks, share, points), f32),
            pltpu.VMEM((groups, regions, share, points), part_kind),
            pltpu.VMEM((groups, regions, share, points), part_kind),
            pltpu.VMEM((regions, share, points), f32),
            pltpu.VMEM((regions, share, points), f32),
        ]
        + [region_dma] * 4 + [group_dma] * 4 + [region_dma] * 2,
        compiler_params=pltpu.CompilerParams(
            collective_id=0, has_side_effects=True, vmem_limit_bytes=56 << 20
        ),
    )(
        sent_slots[0, :, 0],
        many,
        ensemble.reshape(blocks, rows, points),
        increment,
        where,
    )
    return summed / (members * groups - 1)


def solution(mesh):
    in_specs = (
        P("region", "member", None, None),
        P("region", None, None),
        P("region", None, None),
        P("region", None, None),
        P("region", None),
        P("region"),
    )
    out_specs = P("region", "member", None)
    return jax.shard_map(
        per_device, mesh=mesh, in_specs=in_specs, out_specs=out_specs, check_vma=False
    )
```

time: 495 us -> 110 us (0.22)
  starting transfers between devices: 144 us -> 0 us
  waiting for transfers between devices: 105 us -> 0 us
  Pallas kernels: 0 us -> 104 us
  other arithmetic: 97.8 us -> 4.25 us
  matrix products: 82.6 us -> 0 us
  loops' own time: 30.2 us -> 0 us
  local copies, waits for them, and re-layouts: 17.2 us -> 0.68 us
  between operations: 14.1 us -> 0.67 us
    all_to_all x3 -> x0, starting transfers between devices: 144 us -> none  [the longest x1 132 us: per_device(): lax.all_to_all(totals.reshape(regions, per_home, members, levels, points)...]
    pallas_call x0 -> x1, Pallas kernels: none -> 104 us  [per_device(): pl.pallas_call(functools.partial(kernel, regions, groups, levels), out_sh...]
    dot_general x20 -> x0, matrix products: 82.6 us -> none  [the longest x16 54.4 us: diag_one(): lax.dot_general(member_rows, local_tile, (((1,), (1,)), ((), ())), prefer...]
    all_to_all x3 -> x0, waiting for transfers between devices: 73 us -> none  [the longest x1 46.1 us: per_device(): lax.all_to_all(outgoing, 'region', split_axis=0, concat_axis=0, tiled=True)]
    scatter-add x17 -> x0, other arithmetic: 61.9 us -> none  [the longest x8 26.8 us: one_turn(): totals.at[first_slot[within]].add(live_flags[within] * to_first[within])]
    reduce_scatter x1 -> x0, waiting for transfers between devices: 31.9 us -> none  [per_device(): lax.psum_scatter(member_part, 'member', scatter_dimension=1, tiled=True)]
    another operation x2 -> x0, loops' own time: 30.2 us -> none  [the longest x1 30.2 us: pair_terms(): return lax.fori_loop(0, turn_count, one_turn, start_totals)]
    convert_element_type x22 -> x0, other arithmetic: 19.3 us -> none  [the longest x18 11.1 us: tile_of(): left_float = left_where.astype(jnp.float32)]
  transfers between devices with their start and end apart: 4 -> 0, of which waited for: 3 -> 0; matrix products, arithmetic and copies ran while one was open for 16% -> 0% of each run, Pallas kernels for 0% -> 0%
where the time goes in v1:
time: 110 us; the launch traced here: 109 us
  Pallas kernels  104 us (95%)
  other arithmetic  4.25 us (4%)
    pallas_call x1, Pallas kernels, per_device(): pl.pallas_call(functools.partial(kernel, regions, groups, levels), out_sh...  104 us

profile of v1, /device:TPU:1, one launch (start us, length us, event | category | flops | bytes accessed | tf_op | source)
XLA Modules:
  0.0 109.4 jit_solution(1853592923819024304)
XLA Ops:
  0.7 0.7 fusion
  1.4 0.2 convert_reduce_fusion
  1.5 0.7 reshape.42.many_ref
  2.2 1.5 %pad_convert_fusion.where_ref = f32[16,8,512]{2,1,0:T(8,128)} fusion(bf16[16,2,512]{2,1,0:T(2,128)(2,1)} %param.8), kind=kLoop, calls=%fused_computation.1 | loop fusion | flops 65536 | bytes 294912 | tf_op jit(solution)/shard_map/jit(_pad)/pad | solution.py:257
  3.7 103.8 %shard_map.64 = f32[16,16,512]{2,1,0:T(8,128)} custom-call(s32[8]{0:T(128)} %bitcast.5, f32[64]{0:T(128)} %reshape.42.many_ref, bf16[16,256,512]{2,1,0:T(8,128)(2,1)} %bitcast.4, bf16[16,64,512]{2,1,0:T(8,128)(2,1)} %inc_ref.1, f32[16,8,512]{2,1,0:T(8,128)} %pad_convert_fusion.where_ref), custom_call_target="tpu_custom_call" | custom-call | tf_op jit(solution)/shard_map/pallas_call | solution.py:265
  107.5 1.9 %broadcast_multiply_fusion = f32[16,16,512]{2,1,0:T(8,128)} fusion(f32[16,16,512]{2,1,0:T(8,128)} %shard_map.64), kind=kLoop, calls=%fused_computation | loop fusion | flops 131072 | bytes 1048576 | tf_op jit(solution)/shard_map/div | solution.py:297
  (2 shorter events, 0.0 us)

commit v2 on v1

--- a/solution.py
+++ b/solution.py
@@ -8,7 +8,8 @@
 from jax.sharding import PartitionSpec as P
 
 MESH = pl.DeviceIdType.MESH
-ROWS = 32
+ROWS = 64
+PIECE = (16, 256)
 TILE_BYTES = 24 << 20
 
 
@@ -50,10 +51,11 @@
     regions, groups, levels,
     slots_ref, many_ref, ens_ref, inc_ref, where_ref,
     out_ref,
-    place_out, place_in, rows_out, rows_in, weights, field, tiles, square, diag_part, diag_in,
-    pair_part, pair_in, home_out, home_in,
-    place_send, place_recv, rows_send, rows_recv, diag_send, diag_recv, pair_send, pair_recv,
-    home_send, home_recv,
+    place_out, place_in, rows_out, rows_in, inc_out, inc_in, weights, field, tiles, diag_tiles,
+    square, diag_part, diag_in, pair_part, pair_in, home_out, home_in,
+    place_send, place_recv, rows_send, rows_recv, inc_send, inc_recv, home_send, home_recv,
+    half_send, half_recv, diag_send, diag_recv, pair_send, pair_recv,
+    tile_send, tile_recv, own_send, own_recv,
 ):
     blocks, rows, points = ens_ref.shape
     members = rows // levels
@@ -61,16 +63,29 @@
     me = lax.axis_index("region")
     my_group = lax.axis_index("member")
 
-    def to_region(src, dst, send, recv, d):
+    core = lax.rem(my_group, 2)
+    partner = my_group + 1 - 2 * core
+
+    def region_at(step):
+        out, bit = jnp.int32(0), 1
+        while bit < regions:
+            mine, other = lax.rem(lax.div(me, bit), 2), lax.rem(lax.div(jnp.int32(step), bit), 2)
+            out = out + bit * (mine + other - 2 * mine * other)
+            bit *= 2
+        return out
+
+    def to_region(src, dst, send, recv, d, at=None):
         return pltpu.make_async_remote_copy(
-            src_ref=src.at[d], dst_ref=dst.at[d], send_sem=send.at[d], recv_sem=recv.at[d],
-            device_id=(lax.rem(me + d, regions), my_group), device_id_type=MESH,
-        )
-
-    def back_to_region(src, dst, send, recv, d):
+            src_ref=src.at[d], dst_ref=dst.at[d] if at is None else dst.at[d, at],
+            send_sem=send.at[d], recv_sem=recv.at[d],
+            device_id=(region_at(d), my_group), device_id_type=MESH,
+        )
+
+    def to_partner(ref, send, recv, *at):
         return pltpu.make_async_remote_copy(
-            src_ref=src.at[d], dst_ref=dst.at[d], send_sem=send.at[d], recv_sem=recv.at[d],
-            device_id=(lax.rem(me + regions - d, regions), my_group), device_id_type=MESH,
+            src_ref=ref.at[at], dst_ref=ref.at[at],
+            send_sem=send.at[at[0]], recv_sem=recv.at[at[0]],
+            device_id=(me, partner), device_id_type=MESH,
         )
 
     def to_group(src, dst, send, recv, d):
@@ -85,7 +100,7 @@
     @pl.loop(1, regions)
     def _(d):
         pl.semaphore_signal(
-            barrier, inc=1, device_id=(lax.rem(me + d, regions), my_group), device_id_type=MESH
+            barrier, inc=1, device_id=(region_at(d), my_group), device_id_type=MESH
         )
 
     @pl.loop(1, groups)
@@ -94,12 +109,16 @@
             barrier, inc=1, device_id=(me, lax.rem(my_group + d, groups)), device_id_type=MESH
         )
 
+    place_out[...] = jnp.zeros_like(place_out)
     for d in range(regions):
-        slot = slots_ref[lax.rem(me + d, regions)]
+        slot = slots_ref[region_at(d)]
         places, sent = (place_in, rows_in) if d == 0 else (place_out, rows_out)
-        places[d] = where_ref[slot]
-        sent[d, 0:rows] = ens_ref[slot]
-        sent[d, rows : rows + levels] = inc_ref[slot]
+        places[d, 0:2] = where_ref[slot].astype(jnp.float32)
+        sent[d] = ens_ref[slot]
+        if d == 0:
+            inc_in[0] = inc_ref[slot]
+        else:
+            inc_out[d] = inc_ref[slot, core]
     pl.semaphore_wait(barrier, regions + groups - 2)
 
     @pl.loop(1, regions)
@@ -108,10 +127,14 @@
 
     @pl.loop(1, regions)
     def _(d):
+        to_region(inc_out, inc_in, inc_send, inc_recv, d, core).start()
+
+    @pl.loop(1, regions)
+    def _(d):
         to_region(rows_out, rows_in, rows_send, rows_recv, d).start()
 
     def weigh(member_rows, factor):
-        factor = factor.astype(jnp.float32)
+        factor = factor.astype(jnp.float32).reshape(levels, points)
         return jnp.concatenate(
             [
                 (member_rows[m * levels : (m + 1) * levels].astype(jnp.float32) * factor).astype(
@@ -130,24 +153,44 @@
             total = term if total is None else total + term
         return total
 
-    def make_tile(index, left_where, right_where):
+    def make_tile(out, index, left_where, right_where):
         left, _ = left_right(left_where)
         _, right = left_right(right_where)
         square[...] = lax.dot_general(
             left, right, (((0,), (0,)), ((), ())), preferred_element_type=jnp.float32
         )
-
-        @pl.loop(0, points // ROWS)
+        tall, wide = min(ROWS, points), min(PIECE[1], points)
+
+        @pl.loop(0, points // tall)
         def _(step):
-            cut = pl.ds(pl.multiple_of(step * ROWS, ROWS), ROWS)
-            tiles[index, cut] = gaspari_cohn(square[cut])
+            for row in range(0, tall, PIECE[0]):
+                down = pl.ds(pl.multiple_of(step * tall + row, PIECE[0]), PIECE[0])
+                for column in range(0, points, wide):
+                    cut = (down, slice(column, column + wide))
+                    out[(index, *cut)] = gaspari_cohn(square[cut])
+
+    @pl.loop(0, blocks // 2)
+    def _(k):
+        b = 2 * k + core
+        where = where_ref[b].astype(jnp.float32)
+        make_tile(diag_tiles, b, where, where)
+        to_partner(diag_tiles, own_send, own_recv, b).start()
+
+    @pl.loop(1, regions)
+    def _(d):
+        to_region(inc_out, inc_in, inc_send, inc_recv, d, core).wait()
+        to_partner(inc_in, half_send, half_recv, d, core).start()
+
+    @pl.loop(0, blocks // 2)
+    def _(k):
+        to_partner(diag_tiles, own_send, own_recv, 2 * k + core).wait_send()
+        to_partner(diag_tiles, own_send, own_recv, 2 * k + 1 - core).wait_recv()
 
     @pl.loop(0, blocks)
     def _(b):
-        make_tile(0, where_ref[b], where_ref[b])
         member_rows = ens_ref[b]
         results = jnp.dot(
-            weigh(member_rows, inc_ref[b]), tiles[0], preferred_element_type=jnp.float32
+            weigh(member_rows, inc_ref[b]), diag_tiles[b], preferred_element_type=jnp.float32
         )
         total = over_members(member_rows, results)
         for g in range(groups):
@@ -162,30 +205,52 @@
         to_region(place_out, place_in, place_send, place_recv, d).wait()
 
     keep = tiles.shape[0] > 1
-    if keep:
-
+
+    def half_of_pairs(which, do):
         @pl.loop(1, regions)
         def _(v):
-            @pl.loop(0, v)
-            def _(u):
-                make_tile(v * (v - 1) // 2 + u, place_in[u], place_in[v])
+            before = lax.div(v * (v - 1), 2)
+            start = lax.rem(before + which, 2)
+
+            @pl.loop(0, lax.div(v - start + 1, 2))
+            def _(k):
+                u = start + 2 * k
+                do(u, v, before + u)
+
+    def tile_away(u, v, index):
+        make_tile(tiles, index, place_in[u], place_in[v])
+        to_partner(tiles, tile_send, tile_recv, index).start()
+
+    if keep:
+        half_of_pairs(core, tile_away)
+
+    @pl.loop(1, regions)
+    def _(d):
+        to_partner(inc_in, half_send, half_recv, d, core).wait_send()
+        to_partner(inc_in, half_send, half_recv, d, 1 - core).wait_recv()
 
     field[...] = jnp.zeros_like(field)
-    weights[0] = weigh(rows_in[0, 0:rows], rows_in[0, rows : rows + levels])
+    weights[0] = weigh(rows_in[0], inc_in[0])
+
+    if keep:
+        half_of_pairs(core, lambda u, v, i: to_partner(tiles, tile_send, tile_recv, i).wait_send())
+        half_of_pairs(
+            1 - core, lambda u, v, i: to_partner(tiles, tile_send, tile_recv, i).wait_recv()
+        )
 
     @pl.loop(1, regions)
     def _(v):
         to_region(rows_out, rows_in, rows_send, rows_recv, v).wait()
-        weights[v] = weigh(rows_in[v, 0:rows], rows_in[v, rows : rows + levels])
-        second = lax.rem(me + regions - v, regions)
+        weights[v] = weigh(rows_in[v], inc_in[v])
+        second = region_at(v)
 
         @pl.loop(0, v)
         def _(u):
-            first = lax.rem(me + regions - u, regions)
+            first = region_at(u)
             times = many_ref[first * regions + second]
-            index = v * (v - 1) // 2 + u if keep else 0
+            index = lax.div(v * (v - 1), 2) + u if keep else 0
             if not keep:
-                make_tile(0, place_in[u], place_in[v])
+                make_tile(tiles, 0, place_in[u], place_in[v])
             field[u] += times * lax.dot_general(
                 weights[v], tiles[index], (((1,), (1,)), ((), ())),
                 preferred_element_type=jnp.float32,
@@ -196,7 +261,7 @@
 
     @pl.loop(0, regions)
     def _(d):
-        total = over_members(rows_in[d, 0:rows], field[d]).astype(pair_part.dtype)
+        total = over_members(rows_in[d], field[d]).astype(pair_part.dtype)
         for g in range(groups):
             pair_part[g, d] = total[g * share : (g + 1) * share]
 
@@ -216,11 +281,11 @@
         total = pair_part[my_group, d].astype(jnp.float32)
         for g in range(1, groups):
             total = total + pair_in[g, d].astype(jnp.float32)
-        (home_in if d == 0 else home_out)[d] = total
-
-    @pl.loop(1, regions)
-    def _(d):
-        back_to_region(home_out, home_in, home_send, home_recv, d).start()
+        (home_in if d == 0 else home_out)[d] = total.astype(home_in.dtype)
+
+    @pl.loop(1, regions)
+    def _(d):
+        to_region(home_out, home_in, home_send, home_recv, d).start()
 
     @pl.loop(0, blocks)
     def _(b):
@@ -231,14 +296,14 @@
 
     @pl.loop(1, regions)
     def _(d):
-        back_to_region(home_out, home_in, home_send, home_recv, d).wait()
+        to_region(home_out, home_in, home_send, home_recv, d).wait()
 
     @pl.loop(0, blocks)
     def _(b):
         total = out_ref[b]
         for d in range(regions):
-            here = jnp.where(slots_ref[lax.rem(me + d, regions)] == b, 1.0, 0.0)
-            total = total + here * home_in[d]
+            here = jnp.where(slots_ref[region_at(d)] == b, 1.0, 0.0)
+            total = total + here * home_in[d].astype(jnp.float32)
         out_ref[b] = total
 
 
@@ -254,11 +319,11 @@
     first, second = home[:, None, None], home[None, :, None]
     hit = (jnp.minimum(first, second) == low) & (jnp.maximum(first, second) == high) & live
     many = jnp.sum(hit.astype(jnp.float32), axis=2).reshape(regions * regions)
-    where = jnp.pad(coords.astype(jnp.float32), ((0, 0), (0, 6), (0, 0)))
     pairs = regions * (regions - 1) // 2
     tile_total = pairs if pairs * points * points * 2 <= TILE_BYTES else 1
     part_kind = jnp.bfloat16 if share % 16 == 0 else jnp.float32
     vmem, smem = pl.BlockSpec(memory_space=pltpu.VMEM), pl.BlockSpec(memory_space=pltpu.SMEM)
+    half = levels // 2
     region_dma = pltpu.SemaphoreType.DMA((regions,))
     group_dma = pltpu.SemaphoreType.DMA((groups,))
     f32, bf16 = jnp.float32, jnp.bfloat16
@@ -270,20 +335,25 @@
         scratch_shapes=[
             pltpu.VMEM((regions, 8, points), f32),
             pltpu.VMEM((regions, 8, points), f32),
-            pltpu.VMEM((regions, rows + levels, points), bf16),
-            pltpu.VMEM((regions, rows + levels, points), bf16),
+            pltpu.VMEM((regions, rows, points), bf16),
+            pltpu.VMEM((regions, rows, points), bf16),
+            pltpu.VMEM((regions, half, points), bf16),
+            pltpu.VMEM((regions, 2, half, points), bf16),
             pltpu.VMEM((regions, rows, points), bf16),
             pltpu.VMEM((regions, rows, points), f32),
             pltpu.VMEM((tile_total, points, points), bf16),
+            pltpu.VMEM((blocks, points, points), bf16),
             pltpu.VMEM((points, points), f32),
             pltpu.VMEM((groups, blocks, share, points), f32),
             pltpu.VMEM((groups, blocks, share, points), f32),
             pltpu.VMEM((groups, regions, share, points), part_kind),
             pltpu.VMEM((groups, regions, share, points), part_kind),
-            pltpu.VMEM((regions, share, points), f32),
-            pltpu.VMEM((regions, share, points), f32),
+            pltpu.VMEM((regions, share, points), part_kind),
+            pltpu.VMEM((regions, share, points), part_kind),
         ]
-        + [region_dma] * 4 + [group_dma] * 4 + [region_dma] * 2,
+        + [region_dma] * 10 + [group_dma] * 4
+        + [pltpu.SemaphoreType.DMA((tile_total,))] * 2
+        + [pltpu.SemaphoreType.DMA((blocks,))] * 2,
         compiler_params=pltpu.CompilerParams(
             collective_id=0, has_side_effects=True, vmem_limit_bytes=56 << 20
         ),
@@ -291,8 +361,8 @@
         sent_slots[0, :, 0],
         many,
         ensemble.reshape(blocks, rows, points),
-        increment,
-        where,
+        increment.reshape(blocks, 2, half, points),
+        coords,
     )
     return summed / (members * groups - 1)
 

time: 110 us -> 84 us (0.76)
  Pallas kernels: 104 us -> 79.8 us
  other arithmetic: 4.25 us -> 2.76 us
    pallas_call x1, Pallas kernels: 104 us -> 79.8 us  [per_device(): pl.pallas_call(functools.partial(kernel, regions, groups, levels), out_sh...]
    pad x1 -> x0, other arithmetic: 1.49 us -> none  [per_device(): where = jnp.pad(coords.astype(jnp.float32), ((0, 0), (0, 6), (0, 0)))]
where the time goes in v2:
time: 84 us; the launch traced here: 83.9 us
  Pallas kernels  79.8 us (95%)
  other arithmetic  2.76 us (3%)
    pallas_call x1, Pallas kernels, per_device(): pl.pallas_call(functools.partial(kernel, regions, groups, levels), out_sh...  79.8 us
    div x1, other arithmetic, per_device(): return summed / (members * groups - 1)  1.89 us

profile of v2, /device:TPU:1, one launch (start us, length us, event | category | flops | bytes accessed | tf_op | source)
XLA Modules:
  0.0 83.9 jit_solution(1423598310424112976)
XLA Ops:
  0.7 0.7 fusion
  1.4 0.2 convert_reduce_fusion
  1.5 0.6 reshape.45.many_ref
  2.1 79.8 %shard_map.64 = f32[16,16,512]{2,1,0:T(8,128)} custom-call(s32[8]{0:T(128)} %bitcast.7, f32[64]{0:T(128)} %reshape.45.many_ref, bf16[16,256,512]{2,1,0:T(8,128)(2,1)} %bitcast.5, bf16[16,2,32,512]{3,2,1,0:T(8,128)(2,1)} %bitcast.6, bf16[16,2,512]{2,1,0:T(2,128)(2,1)} %where_ref.1), custom_call_target="tpu_custom_call" | custom-call | tf_op jit(solution)/shard_map/pallas_call | solution.py:330
  82.0 1.9 %broadcast_multiply_fusion = f32[16,16,512]{2,1,0:T(8,128)} fusion(f32[16,16,512]{2,1,0:T(8,128)} %shard_map.64), kind=kLoop, calls=%fused_computation | loop fusion | flops 131072 | bytes 1048576 | tf_op jit(solution)/shard_map/div | solution.py:367
  (2 shorter events, 0.0 us)

commit v3 on v2

--- a/solution.py
+++ b/solution.py
@@ -49,7 +49,7 @@
 
 def kernel(
     regions, groups, levels,
-    slots_ref, many_ref, ens_ref, inc_ref, where_ref,
+    slots_ref, count_ref, list_ref, ens_ref, inc_ref, where_ref,
     out_ref,
     place_out, place_in, rows_out, rows_in, inc_out, inc_in, weights, field, tiles, diag_tiles,
     square, diag_part, diag_in, pair_part, pair_in, home_out, home_in,
@@ -111,7 +111,7 @@
 
     place_out[...] = jnp.zeros_like(place_out)
     for d in range(regions):
-        slot = slots_ref[region_at(d)]
+        slot = slots_ref[0, region_at(d), 0]
         places, sent = (place_in, rows_in) if d == 0 else (place_out, rows_out)
         places[d, 0:2] = where_ref[slot].astype(jnp.float32)
         sent[d] = ens_ref[slot]
@@ -129,9 +129,18 @@
     def _(d):
         to_region(inc_out, inc_in, inc_send, inc_recv, d, core).start()
 
-    @pl.loop(1, regions)
-    def _(d):
-        to_region(rows_out, rows_in, rows_send, rows_recv, d).start()
+    stages = [range(regions // 2, 3 * regions // 4), range(1, regions // 2)]
+    later = [
+        range(3 * regions // 4, 7 * regions // 8), range(7 * regions // 8, regions)
+    ] if regions % 8 == 0 else [range(3 * regions // 4, regions), range(0)]
+
+    def send_rows(steps):
+        @pl.loop(steps.start, steps.stop)
+        def _(d):
+            to_region(rows_out, rows_in, rows_send, rows_recv, d).start()
+
+    for steps in stages:
+        send_rows(steps)
 
     def weigh(member_rows, factor):
         factor = factor.astype(jnp.float32).reshape(levels, points)
@@ -153,28 +162,51 @@
             total = term if total is None else total + term
         return total
 
-    def make_tile(out, index, left_where, right_where):
+    def squares(left_where, right_where):
         left, _ = left_right(left_where)
         _, right = left_right(right_where)
         square[...] = lax.dot_general(
             left, right, (((0,), (0,)), ((), ())), preferred_element_type=jnp.float32
         )
-        tall, wide = min(ROWS, points), min(PIECE[1], points)
-
-        @pl.loop(0, points // tall)
+
+    def fill(size, parts):
+        tall, wide = min(ROWS, size), min(PIECE[1], size)
+
+        @pl.loop(0, size // tall)
         def _(step):
             for row in range(0, tall, PIECE[0]):
-                down = pl.ds(pl.multiple_of(step * tall + row, PIECE[0]), PIECE[0])
-                for column in range(0, points, wide):
-                    cut = (down, slice(column, column + wide))
-                    out[(index, *cut)] = gaspari_cohn(square[cut])
+                down = pl.multiple_of(step * tall + row, PIECE[0])
+                for out, at, top, side in parts:
+                    for column in range(0, size, wide):
+                        out[(*at, pl.ds(down, PIECE[0]), slice(column, column + wide))] = gaspari_cohn(
+                            square[
+                                pl.ds(pl.multiple_of(down + top, PIECE[0]), PIECE[0]),
+                                side + column : side + column + wide,
+                            ]
+                        )
+
+    def make_tile(out, index, left_where, right_where):
+        squares(left_where, right_where)
+        fill(points, [(out, (index,), 0, 0)])
+
+    half = points // 2
 
     @pl.loop(0, blocks // 2)
     def _(k):
         b = 2 * k + core
         where = where_ref[b].astype(jnp.float32)
-        make_tile(diag_tiles, b, where, where)
+        squares(where, where)
+        fill(
+            half,
+            [
+                (diag_tiles, (b, 0), 0, 0),
+                (diag_tiles, (b, 1), 0, half),
+                (diag_tiles, (b, 2), half, half),
+            ],
+        )
         to_partner(diag_tiles, own_send, own_recv, b).start()
+
+    send_rows(later[0])
 
     @pl.loop(1, regions)
     def _(d):
@@ -189,8 +221,19 @@
     @pl.loop(0, blocks)
     def _(b):
         member_rows = ens_ref[b]
-        results = jnp.dot(
-            weigh(member_rows, inc_ref[b]), diag_tiles[b], preferred_element_type=jnp.float32
+        weighted = weigh(member_rows, inc_ref[b])
+        first, second = weighted[:, :half], weighted[:, half:]
+        corner = diag_tiles[b, 1]
+        results = jnp.concatenate(
+            [
+                jnp.dot(first, diag_tiles[b, 0], preferred_element_type=jnp.float32)
+                + lax.dot_general(
+                    second, corner, (((1,), (1,)), ((), ())), preferred_element_type=jnp.float32
+                ),
+                jnp.dot(first, corner, preferred_element_type=jnp.float32)
+                + jnp.dot(second, diag_tiles[b, 2], preferred_element_type=jnp.float32),
+            ],
+            1,
         )
         total = over_members(member_rows, results)
         for g in range(groups):
@@ -199,6 +242,8 @@
     @pl.loop(1, groups)
     def _(d):
         to_group(diag_part, diag_in, diag_send, diag_recv, d).start()
+
+    send_rows(later[1])
 
     @pl.loop(1, regions)
     def _(d):
@@ -229,6 +274,10 @@
         to_partner(inc_in, half_send, half_recv, d, core).wait_send()
         to_partner(inc_in, half_send, half_recv, d, 1 - core).wait_recv()
 
+    one_end, other_end = list_ref[:, 0:1], list_ref[:, 1:2]
+    alive = jnp.where(
+        lax.broadcasted_iota(jnp.int32, one_end.shape, 0) < count_ref[0], 1.0, 0.0
+    )
     field[...] = jnp.zeros_like(field)
     weights[0] = weigh(rows_in[0], inc_in[0])
 
@@ -247,7 +296,12 @@
         @pl.loop(0, v)
         def _(u):
             first = region_at(u)
-            times = many_ref[first * regions + second]
+            listed = ((one_end == first) & (other_end == second)) | (
+                (one_end == second) & (other_end == first)
+            )
+            times = jnp.sum(
+                jnp.where(listed, alive, 0.0), axis=0, keepdims=True
+            )
             index = lax.div(v * (v - 1), 2) + u if keep else 0
             if not keep:
                 make_tile(tiles, 0, place_in[u], place_in[v])
@@ -277,15 +331,13 @@
     def _(d):
         to_group(pair_part, pair_in, pair_send, pair_recv, d).wait()
 
-    for d in range(regions):
+    for d in reversed(range(regions)):
         total = pair_part[my_group, d].astype(jnp.float32)
         for g in range(1, groups):
             total = total + pair_in[g, d].astype(jnp.float32)
         (home_in if d == 0 else home_out)[d] = total.astype(home_in.dtype)
-
-    @pl.loop(1, regions)
-    def _(d):
-        to_region(home_out, home_in, home_send, home_recv, d).start()
+        if d > 0:
+            to_region(home_out, home_in, home_send, home_recv, d).start()
 
     @pl.loop(0, blocks)
     def _(b):
@@ -302,7 +354,7 @@
     def _(b):
         total = out_ref[b]
         for d in range(regions):
-            here = jnp.where(slots_ref[region_at(d)] == b, 1.0, 0.0)
+            here = jnp.where(slots_ref[0, region_at(d), 0] == b, 1.0, 0.0)
             total = total + here * home_in[d].astype(jnp.float32)
         out_ref[b] = total
 
@@ -312,13 +364,6 @@
     regions, groups = lax.axis_size("region"), lax.axis_size("member")
     share = levels // groups
     rows = members * levels
-    live = jnp.arange(pair_list.shape[0], dtype=jnp.int32) < pair_count[0]
-    low = jnp.min(pair_list, axis=1)
-    high = jnp.max(pair_list, axis=1)
-    home = jnp.arange(regions, dtype=jnp.int32)
-    first, second = home[:, None, None], home[None, :, None]
-    hit = (jnp.minimum(first, second) == low) & (jnp.maximum(first, second) == high) & live
-    many = jnp.sum(hit.astype(jnp.float32), axis=2).reshape(regions * regions)
     pairs = regions * (regions - 1) // 2
     tile_total = pairs if pairs * points * points * 2 <= TILE_BYTES else 1
     part_kind = jnp.bfloat16 if share % 16 == 0 else jnp.float32
@@ -330,7 +375,7 @@
     summed = pl.pallas_call(
         functools.partial(kernel, regions, groups, levels),
         out_shape=jax.ShapeDtypeStruct((blocks, share, points), f32),
-        in_specs=[smem, smem, vmem, vmem, vmem],
+        in_specs=[smem, smem, vmem, vmem, vmem, vmem],
         out_specs=vmem,
         scratch_shapes=[
             pltpu.VMEM((regions, 8, points), f32),
@@ -342,7 +387,7 @@
             pltpu.VMEM((regions, rows, points), bf16),
             pltpu.VMEM((regions, rows, points), f32),
             pltpu.VMEM((tile_total, points, points), bf16),
-            pltpu.VMEM((blocks, points, points), bf16),
+            pltpu.VMEM((blocks, 3, points // 2, points // 2), bf16),
             pltpu.VMEM((points, points), f32),
             pltpu.VMEM((groups, blocks, share, points), f32),
             pltpu.VMEM((groups, blocks, share, points), f32),
@@ -358,8 +403,9 @@
             collective_id=0, has_side_effects=True, vmem_limit_bytes=56 << 20
         ),
     )(
-        sent_slots[0, :, 0],
-        many,
+        sent_slots,
+        pair_count,
+        pair_list,
         ensemble.reshape(blocks, rows, points),
         increment.reshape(blocks, 2, half, points),
         coords,

time: 84 us -> 88 us (1.048)
  Pallas kernels: 79.8 us -> 82.6 us
  local copies, waits for them, and re-layouts: 0.6 us -> 2.67 us
    pallas_call x1, Pallas kernels: 79.8 us -> 82.6 us  [per_device(): pl.pallas_call(functools.partial(kernel, regions, groups, levels), out_sh...]
    unnamed x0 -> x2, local copies, waits for them, and re-layouts: none -> 2.67 us
where the time goes in v3:
time: 88 us; the launch traced here: 87.8 us
  Pallas kernels  82.6 us (94%)
  local copies, waits for them, and re-layouts  2.67 us (3%)
  other arithmetic  1.89 us (2%)
    pallas_call x1, Pallas kernels, per_device(): pl.pallas_call(functools.partial(kernel, regions, groups, levels), out_sh...  82.6 us
    unnamed x2, local copies, waits for them, and re-layouts  2.67 us
    div x1, other arithmetic, per_device(): return summed / (members * groups - 1)  1.89 us

profile of v3, /device:TPU:1, one launch (start us, length us, event | category | flops | bytes accessed | tf_op | source)
XLA Modules:
  0.0 87.8 jit_solution(6201856285900491527)
XLA Ops:
  0.7 1.3 %copy.7.slots_ref = s32[1,8,1]{2,1,0:T(8,128)} copy(s32[1,8,1]{1,2,0:T(1,128)} %param.9) | data formatting | bytes 64 | tf_op args[3]
  2.0 1.4 %copy.8.list_ref = s32[16,2]{1,0:T(8,128)} copy(s32[16,2]{0,1:T(2,128)} %param.10) | data formatting | bytes 256 | tf_op args[4]
  3.3 82.6 %shard_map.64 = f32[16,16,512]{2,1,0:T(8,128)} custom-call(s32[1,8,1]{2,1,0:T(8,128)} %copy.7.slots_ref, s32[1]{0:T(128)S(6)} %copy.9.count_ref, s32[16,2]{1,0:T(8,128)} %copy.8.list_ref, bf16[16,256,512]{2,1,0:T(8,128)(2,1)} %bitcast.2, bf16[16,2,32,512]{3,2,1,0:T(8,128)(2,1)} %bitcast.3, bf16[16,2,512]{2,1,0:T(2,128)(2,1)} %where_ref.1), custom_call_target="tpu_custom_call" | custom-call | tf_op jit(solution)/shard_map/pallas_call | solution.py:375
  86.0 1.9 %broadcast_multiply_fusion = f32[16,16,512]{2,1,0:T(8,128)} fusion(f32[16,16,512]{2,1,0:T(8,128)} %shard_map.64), kind=kLoop, calls=%fused_computation | loop fusion | flops 131072 | bytes 1048576 | tf_op jit(solution)/shard_map/div | solution.py:413

commit v4 on v3

--- a/solution.py
+++ b/solution.py
@@ -33,7 +33,7 @@
     )
 
 
-def gaspari_cohn(square):
+def gaspari_cohn(square, scale=1.0 / 12.0):
     square = jnp.maximum(square, 2.0**-10)
     inverse = lax.rsqrt(square)
     z = square * inverse
@@ -44,12 +44,12 @@
     near = near + near
     both = square + z
     total = (far * far) * (both + (z - 0.5)) + (near * near) * (2.0 - both)
-    return (total * (inverse * (1.0 / 12.0))).astype(jnp.bfloat16)
+    return (total * (inverse * scale)).astype(jnp.bfloat16)
 
 
 def kernel(
     regions, groups, levels,
-    slots_ref, count_ref, list_ref, ens_ref, inc_ref, where_ref,
+    slots_ref, many_ref, ens_ref, inc_ref, where_ref,
     out_ref,
     place_out, place_in, rows_out, rows_in, inc_out, inc_in, weights, field, tiles, diag_tiles,
     square, diag_part, diag_in, pair_part, pair_in, home_out, home_in,
@@ -111,7 +111,7 @@
 
     place_out[...] = jnp.zeros_like(place_out)
     for d in range(regions):
-        slot = slots_ref[0, region_at(d), 0]
+        slot = slots_ref[region_at(d)]
         places, sent = (place_in, rows_in) if d == 0 else (place_out, rows_out)
         places[d, 0:2] = where_ref[slot].astype(jnp.float32)
         sent[d] = ens_ref[slot]
@@ -129,18 +129,13 @@
     def _(d):
         to_region(inc_out, inc_in, inc_send, inc_recv, d, core).start()
 
-    stages = [range(regions // 2, 3 * regions // 4), range(1, regions // 2)]
-    later = [
-        range(3 * regions // 4, 7 * regions // 8), range(7 * regions // 8, regions)
-    ] if regions % 8 == 0 else [range(3 * regions // 4, regions), range(0)]
-
     def send_rows(steps):
         @pl.loop(steps.start, steps.stop)
         def _(d):
             to_region(rows_out, rows_in, rows_send, rows_recv, d).start()
 
-    for steps in stages:
-        send_rows(steps)
+    send_rows(range(regions // 2, regions))
+    send_rows(range(1, regions // 2))
 
     def weigh(member_rows, factor):
         factor = factor.astype(jnp.float32).reshape(levels, points)
@@ -169,25 +164,33 @@
             left, right, (((0,), (0,)), ((), ())), preferred_element_type=jnp.float32
         )
 
-    def fill(size, parts):
+    def fill(size, parts, scale=1.0 / 12.0, unroll=False):
         tall, wide = min(ROWS, size), min(PIECE[1], size)
 
-        @pl.loop(0, size // tall)
-        def _(step):
+        def some_rows(step):
             for row in range(0, tall, PIECE[0]):
-                down = pl.multiple_of(step * tall + row, PIECE[0])
+                down = step * tall + row
+                if not unroll:
+                    down = pl.multiple_of(down, PIECE[0])
                 for out, at, top, side in parts:
                     for column in range(0, size, wide):
                         out[(*at, pl.ds(down, PIECE[0]), slice(column, column + wide))] = gaspari_cohn(
                             square[
-                                pl.ds(pl.multiple_of(down + top, PIECE[0]), PIECE[0]),
-                                side + column : side + column + wide,
-                            ]
+                                pl.ds(down + top, PIECE[0]), side + column : side + column + wide
+                            ],
+                            scale,
                         )
 
-    def make_tile(out, index, left_where, right_where):
-        squares(left_where, right_where)
-        fill(points, [(out, (index,), 0, 0)])
+        if unroll:
+            for step in range(size // tall):
+                some_rows(step)
+        else:
+            pl.loop(0, size // tall)(some_rows)
+
+    def make_pair_tile(index, u, v, unroll):
+        squares(place_in[u], place_in[v])
+        times = many_ref[region_at(u) * regions + region_at(v)]
+        fill(points, [(tiles, (index,), 0, 0)], times * (1.0 / 12.0), unroll)
 
     half = points // 2
 
@@ -206,8 +209,6 @@
         )
         to_partner(diag_tiles, own_send, own_recv, b).start()
 
-    send_rows(later[0])
-
     @pl.loop(1, regions)
     def _(d):
         to_region(inc_out, inc_in, inc_send, inc_recv, d, core).wait()
@@ -218,8 +219,7 @@
         to_partner(diag_tiles, own_send, own_recv, 2 * k + core).wait_send()
         to_partner(diag_tiles, own_send, own_recv, 2 * k + 1 - core).wait_recv()
 
-    @pl.loop(0, blocks)
-    def _(b):
+    def diag_product(b):
         member_rows = ens_ref[b]
         weighted = weigh(member_rows, inc_ref[b])
         first, second = weighted[:, :half], weighted[:, half:]
@@ -239,12 +239,6 @@
         for g in range(groups):
             diag_part[g, b] = total[g * share : (g + 1) * share]
 
-    @pl.loop(1, groups)
-    def _(d):
-        to_group(diag_part, diag_in, diag_send, diag_recv, d).start()
-
-    send_rows(later[1])
-
     @pl.loop(1, regions)
     def _(d):
         to_region(place_out, place_in, place_send, place_recv, d).wait()
@@ -263,21 +257,25 @@
                 do(u, v, before + u)
 
     def tile_away(u, v, index):
-        make_tile(tiles, index, place_in[u], place_in[v])
+        make_pair_tile(index, u, v, True)
+        diag_product(lax.div(index, 2))
         to_partner(tiles, tile_send, tile_recv, index).start()
 
+    done = 0
     if keep:
         half_of_pairs(core, tile_away)
+        done = tiles.shape[0] // 2
+    pl.loop(done, blocks)(diag_product)
+
+    @pl.loop(1, groups)
+    def _(d):
+        to_group(diag_part, diag_in, diag_send, diag_recv, d).start()
 
     @pl.loop(1, regions)
     def _(d):
         to_partner(inc_in, half_send, half_recv, d, core).wait_send()
         to_partner(inc_in, half_send, half_recv, d, 1 - core).wait_recv()
 
-    one_end, other_end = list_ref[:, 0:1], list_ref[:, 1:2]
-    alive = jnp.where(
-        lax.broadcasted_iota(jnp.int32, one_end.shape, 0) < count_ref[0], 1.0, 0.0
-    )
     field[...] = jnp.zeros_like(field)
     weights[0] = weigh(rows_in[0], inc_in[0])
 
@@ -291,27 +289,17 @@
     def _(v):
         to_region(rows_out, rows_in, rows_send, rows_recv, v).wait()
         weights[v] = weigh(rows_in[v], inc_in[v])
-        second = region_at(v)
 
         @pl.loop(0, v)
         def _(u):
-            first = region_at(u)
-            listed = ((one_end == first) & (other_end == second)) | (
-                (one_end == second) & (other_end == first)
-            )
-            times = jnp.sum(
-                jnp.where(listed, alive, 0.0), axis=0, keepdims=True
-            )
             index = lax.div(v * (v - 1), 2) + u if keep else 0
             if not keep:
-                make_tile(tiles, 0, place_in[u], place_in[v])
-            field[u] += times * lax.dot_general(
+                make_pair_tile(0, u, v, False)
+            field[u] += lax.dot_general(
                 weights[v], tiles[index], (((1,), (1,)), ((), ())),
                 preferred_element_type=jnp.float32,
             )
-            field[v] += times * jnp.dot(
-                weights[u], tiles[index], preferred_element_type=jnp.float32
-            )
+            field[v] += jnp.dot(weights[u], tiles[index], preferred_element_type=jnp.float32)
 
     @pl.loop(0, regions)
     def _(d):
@@ -354,7 +342,7 @@
     def _(b):
         total = out_ref[b]
         for d in range(regions):
-            here = jnp.where(slots_ref[0, region_at(d), 0] == b, 1.0, 0.0)
+            here = jnp.where(slots_ref[region_at(d)] == b, 1.0, 0.0)
             total = total + here * home_in[d].astype(jnp.float32)
         out_ref[b] = total
 
@@ -364,8 +352,14 @@
     regions, groups = lax.axis_size("region"), lax.axis_size("member")
     share = levels // groups
     rows = members * levels
+    live = jnp.arange(pair_list.shape[0], dtype=jnp.int32) < pair_count[0]
+    low, high = jnp.min(pair_list, axis=1), jnp.max(pair_list, axis=1)
+    home = jnp.arange(regions, dtype=jnp.int32)
+    first, second = home[:, None, None], home[None, :, None]
+    hit = (jnp.minimum(first, second) == low) & (jnp.maximum(first, second) == high) & live
+    many = jnp.sum(hit.astype(jnp.float32), axis=2).reshape(regions * regions)
     pairs = regions * (regions - 1) // 2
-    tile_total = pairs if pairs * points * points * 2 <= TILE_BYTES else 1
+    tile_total = pairs if pairs * points * points * 2 <= TILE_BYTES and pairs <= 2 * blocks else 1
     part_kind = jnp.bfloat16 if share % 16 == 0 else jnp.float32
     vmem, smem = pl.BlockSpec(memory_space=pltpu.VMEM), pl.BlockSpec(memory_space=pltpu.SMEM)
     half = levels // 2
@@ -375,7 +369,7 @@
     summed = pl.pallas_call(
         functools.partial(kernel, regions, groups, levels),
         out_shape=jax.ShapeDtypeStruct((blocks, share, points), f32),
-        in_specs=[smem, smem, vmem, vmem, vmem, vmem],
+        in_specs=[smem, smem, vmem, vmem, vmem],
         out_specs=vmem,
         scratch_shapes=[
             pltpu.VMEM((regions, 8, points), f32),
@@ -403,9 +397,8 @@
             collective_id=0, has_side_effects=True, vmem_limit_bytes=56 << 20
         ),
     )(
-        sent_slots,
-        pair_count,
-        pair_list,
+        sent_slots[0, :, 0],
+        many,
         ensemble.reshape(blocks, rows, points),
         increment.reshape(blocks, 2, half, points),
         coords,

time: 88 us -> 96.7 us (1.099)
  Pallas kernels: 82.6 us -> 92.5 us
  local copies, waits for them, and re-layouts: 2.67 us -> 0.6 us
    pallas_call x1, Pallas kernels: 82.6 us -> 92.5 us  [per_device(): pl.pallas_call(functools.partial(kernel, regions, groups, levels), out_sh...]
    unnamed x2 -> x0, local copies, waits for them, and re-layouts: 2.67 us -> none
where the time goes in v4:
time: 96.7 us; the launch traced here: 96.5 us
  Pallas kernels  92.5 us (96%)
  other arithmetic  2.76 us (3%)
    pallas_call x1, Pallas kernels, per_device(): pl.pallas_call(functools.partial(kernel, regions, groups, levels), out_sh...  92.5 us

profile of v4, /device:TPU:1, one launch (start us, length us, event | category | flops | bytes accessed | tf_op | source)
XLA Modules:
  0.0 96.5 jit_solution(12173885818205722842)
XLA Ops:
  0.7 0.7 fusion
  1.4 0.2 convert_reduce_fusion
  1.5 0.6 reshape.45.many_ref
  2.1 92.5 %shard_map.64 = f32[16,16,512]{2,1,0:T(8,128)} custom-call(s32[8]{0:T(128)} %bitcast.7, f32[64]{0:T(128)} %reshape.45.many_ref, bf16[16,256,512]{2,1,0:T(8,128)(2,1)} %bitcast.5, bf16[16,2,32,512]{3,2,1,0:T(8,128)(2,1)} %bitcast.6, bf16[16,2,512]{2,1,0:T(2,128)(2,1)} %where_ref.1), custom_call_target="tpu_custom_call" | custom-call | tf_op jit(solution)/shard_map/pallas_call | solution.py:369
  94.6 1.9 %broadcast_multiply_fusion = f32[16,16,512]{2,1,0:T(8,128)} fusion(f32[16,16,512]{2,1,0:T(8,128)} %shard_map.64), kind=kLoop, calls=%fused_computation | loop fusion | flops 131072 | bytes 1048576 | tf_op jit(solution)/shard_map/div | solution.py:406
  (2 shorter events, 0.0 us)

commit v5 on v4

--- a/solution.py
+++ b/solution.py
@@ -74,6 +74,13 @@
             bit *= 2
         return out
 
+    def turn(t):
+        t = jnp.int32(t)
+        others = regions - 1
+        some = lax.div(t + others, regions)
+        near = regions // 2 - 1
+        return some * (lax.rem(t - 1 + others + core * near, others) + 1)
+
     def to_region(src, dst, send, recv, d, at=None):
         return pltpu.make_async_remote_copy(
             src_ref=src.at[d], dst_ref=dst.at[d] if at is None else dst.at[d, at],
@@ -129,13 +136,9 @@
     def _(d):
         to_region(inc_out, inc_in, inc_send, inc_recv, d, core).start()
 
-    def send_rows(steps):
-        @pl.loop(steps.start, steps.stop)
-        def _(d):
-            to_region(rows_out, rows_in, rows_send, rows_recv, d).start()
-
-    send_rows(range(regions // 2, regions))
-    send_rows(range(1, regions // 2))
+    @pl.loop(1, regions)
+    def _(t):
+        to_region(rows_out, rows_in, rows_send, rows_recv, turn(t)).start()
 
     def weigh(member_rows, factor):
         factor = factor.astype(jnp.float32).reshape(levels, points)
@@ -164,33 +167,27 @@
             left, right, (((0,), (0,)), ((), ())), preferred_element_type=jnp.float32
         )
 
-    def fill(size, parts, scale=1.0 / 12.0, unroll=False):
+    def fill(size, parts, scale=1.0 / 12.0):
         tall, wide = min(ROWS, size), min(PIECE[1], size)
 
         def some_rows(step):
             for row in range(0, tall, PIECE[0]):
-                down = step * tall + row
-                if not unroll:
-                    down = pl.multiple_of(down, PIECE[0])
+                down = pl.multiple_of(step * tall + row, PIECE[0])
                 for out, at, top, side in parts:
                     for column in range(0, size, wide):
                         out[(*at, pl.ds(down, PIECE[0]), slice(column, column + wide))] = gaspari_cohn(
                             square[
-                                pl.ds(down + top, PIECE[0]), side + column : side + column + wide
+                                pl.ds(pl.multiple_of(down + top, PIECE[0]), PIECE[0]), side + column : side + column + wide
                             ],
                             scale,
                         )
 
-        if unroll:
-            for step in range(size // tall):
-                some_rows(step)
-        else:
-            pl.loop(0, size // tall)(some_rows)
-
-    def make_pair_tile(index, u, v, unroll):
+        pl.loop(0, size // tall)(some_rows)
+
+    def make_pair_tile(index, u, v):
         squares(place_in[u], place_in[v])
         times = many_ref[region_at(u) * regions + region_at(v)]
-        fill(points, [(tiles, (index,), 0, 0)], times * (1.0 / 12.0), unroll)
+        fill(points, [(tiles, (index,), 0, 0)], times * (1.0 / 12.0))
 
     half = points // 2
 
@@ -219,7 +216,8 @@
         to_partner(diag_tiles, own_send, own_recv, 2 * k + core).wait_send()
         to_partner(diag_tiles, own_send, own_recv, 2 * k + 1 - core).wait_recv()
 
-    def diag_product(b):
+    @pl.loop(0, blocks)
+    def _(b):
         member_rows = ens_ref[b]
         weighted = weigh(member_rows, inc_ref[b])
         first, second = weighted[:, :half], weighted[:, half:]
@@ -239,6 +237,10 @@
         for g in range(groups):
             diag_part[g, b] = total[g * share : (g + 1) * share]
 
+    @pl.loop(1, groups)
+    def _(d):
+        to_group(diag_part, diag_in, diag_send, diag_recv, d).start()
+
     @pl.loop(1, regions)
     def _(d):
         to_region(place_out, place_in, place_send, place_recv, d).wait()
@@ -257,19 +259,11 @@
                 do(u, v, before + u)
 
     def tile_away(u, v, index):
-        make_pair_tile(index, u, v, True)
-        diag_product(lax.div(index, 2))
+        make_pair_tile(index, u, v)
         to_partner(tiles, tile_send, tile_recv, index).start()
 
-    done = 0
     if keep:
         half_of_pairs(core, tile_away)
-        done = tiles.shape[0] // 2
-    pl.loop(done, blocks)(diag_product)
-
-    @pl.loop(1, groups)
-    def _(d):
-        to_group(diag_part, diag_in, diag_send, diag_recv, d).start()
 
     @pl.loop(1, regions)
     def _(d):
@@ -286,15 +280,20 @@
         )
 
     @pl.loop(1, regions)
-    def _(v):
-        to_region(rows_out, rows_in, rows_send, rows_recv, v).wait()
-        weights[v] = weigh(rows_in[v], inc_in[v])
-
-        @pl.loop(0, v)
-        def _(u):
+    def _(t):
+        late = turn(t)
+        to_region(rows_out, rows_in, rows_send, rows_recv, late).wait()
+        weights[late] = weigh(rows_in[late], inc_in[late])
+
+        @pl.loop(0, t)
+        def _(before):
+            early = turn(before)
+            up = lax.div(late - early + regions, regions)
+            v = up * late + (1 - up) * early
+            u = late + early - v
             index = lax.div(v * (v - 1), 2) + u if keep else 0
             if not keep:
-                make_pair_tile(0, u, v, False)
+                make_pair_tile(0, u, v)
             field[u] += lax.dot_general(
                 weights[v], tiles[index], (((1,), (1,)), ((), ())),
                 preferred_element_type=jnp.float32,

time: 96.7 us -> 89 us (0.920)
  Pallas kernels: 92.5 us -> 84.7 us
    pallas_call x1, Pallas kernels: 92.5 us -> 84.7 us  [per_device(): pl.pallas_call(functools.partial(kernel, regions, groups, levels), out_sh...]
where the time goes in v5:
time: 89 us; the launch traced here: 88.8 us
  Pallas kernels  84.7 us (95%)
  other arithmetic  2.76 us (3%)
    pallas_call x1, Pallas kernels, per_device(): pl.pallas_call(functools.partial(kernel, regions, groups, levels), out_sh...  84.7 us
    div x1, other arithmetic, per_device(): return summed / (members * groups - 1)  1.89 us

profile of v5, /device:TPU:1, one launch (start us, length us, event | category | flops | bytes accessed | tf_op | source)
XLA Modules:
  0.0 88.8 jit_solution(9559953948794724624)
XLA Ops:
  0.7 0.7 fusion
  1.4 0.2 convert_reduce_fusion
  1.5 0.6 reshape.45.many_ref
  2.1 84.7 %shard_map.64 = f32[16,16,512]{2,1,0:T(8,128)} custom-call(s32[8]{0:T(128)} %bitcast.7, f32[64]{0:T(128)} %reshape.45.many_ref, bf16[16,256,512]{2,1,0:T(8,128)(2,1)} %bitcast.5, bf16[16,2,32,512]{3,2,1,0:T(8,128)(2,1)} %bitcast.6, bf16[16,2,512]{2,1,0:T(2,128)(2,1)} %where_ref.1), custom_call_target="tpu_custom_call" | custom-call | tf_op jit(solution)/shard_map/pallas_call | solution.py:368
  86.9 1.9 %broadcast_multiply_fusion = f32[16,16,512]{2,1,0:T(8,128)} fusion(f32[16,16,512]{2,1,0:T(8,128)} %shard_map.64), kind=kLoop, calls=%fused_computation | loop fusion | flops 131072 | bytes 1048576 | tf_op jit(solution)/shard_map/div | solution.py:405
  (2 shorter events, 0.0 us)

commit v6 on v2

--- a/solution.py
+++ b/solution.py
@@ -33,7 +33,7 @@
     )
 
 
-def gaspari_cohn(square):
+def gaspari_cohn(square, scale):
     square = jnp.maximum(square, 2.0**-10)
     inverse = lax.rsqrt(square)
     z = square * inverse
@@ -44,7 +44,7 @@
     near = near + near
     both = square + z
     total = (far * far) * (both + (z - 0.5)) + (near * near) * (2.0 - both)
-    return (total * (inverse * (1.0 / 12.0))).astype(jnp.bfloat16)
+    return (total * (inverse * scale)).astype(jnp.bfloat16)
 
 
 def kernel(
@@ -153,13 +153,14 @@
             total = term if total is None else total + term
         return total
 
-    def make_tile(out, index, left_where, right_where):
+    def make_tile(out, index, left_where, right_where, times=1.0):
         left, _ = left_right(left_where)
         _, right = left_right(right_where)
         square[...] = lax.dot_general(
             left, right, (((0,), (0,)), ((), ())), preferred_element_type=jnp.float32
         )
         tall, wide = min(ROWS, points), min(PIECE[1], points)
+        scale = times * (1.0 / 12.0)
 
         @pl.loop(0, points // tall)
         def _(step):
@@ -167,7 +168,7 @@
                 down = pl.ds(pl.multiple_of(step * tall + row, PIECE[0]), PIECE[0])
                 for column in range(0, points, wide):
                     cut = (down, slice(column, column + wide))
-                    out[(index, *cut)] = gaspari_cohn(square[cut])
+                    out[(index, *cut)] = gaspari_cohn(square[cut], scale)
 
     @pl.loop(0, blocks // 2)
     def _(k):
@@ -217,8 +218,12 @@
                 u = start + 2 * k
                 do(u, v, before + u)
 
+    def pair_tile(index, u, v):
+        times = many_ref[region_at(u) * regions + region_at(v)]
+        make_tile(tiles, index, place_in[u], place_in[v], times)
+
     def tile_away(u, v, index):
-        make_tile(tiles, index, place_in[u], place_in[v])
+        pair_tile(index, u, v)
         to_partner(tiles, tile_send, tile_recv, index).start()
 
     if keep:
@@ -242,22 +247,17 @@
     def _(v):
         to_region(rows_out, rows_in, rows_send, rows_recv, v).wait()
         weights[v] = weigh(rows_in[v], inc_in[v])
-        second = region_at(v)
 
         @pl.loop(0, v)
         def _(u):
-            first = region_at(u)
-            times = many_ref[first * regions + second]
             index = lax.div(v * (v - 1), 2) + u if keep else 0
             if not keep:
-                make_tile(tiles, 0, place_in[u], place_in[v])
-            field[u] += times * lax.dot_general(
+                pair_tile(0, u, v)
+            field[u] += lax.dot_general(
                 weights[v], tiles[index], (((1,), (1,)), ((), ())),
                 preferred_element_type=jnp.float32,
             )
-            field[v] += times * jnp.dot(
-                weights[u], tiles[index], preferred_element_type=jnp.float32
-            )
+            field[v] += jnp.dot(weights[u], tiles[index], preferred_element_type=jnp.float32)
 
     @pl.loop(0, regions)
     def _(d):
@@ -277,15 +277,13 @@
     def _(d):
         to_group(pair_part, pair_in, pair_send, pair_recv, d).wait()
 
-    for d in range(regions):
+    for d in reversed(range(regions)):
         total = pair_part[my_group, d].astype(jnp.float32)
         for g in range(1, groups):
             total = total + pair_in[g, d].astype(jnp.float32)
         (home_in if d == 0 else home_out)[d] = total.astype(home_in.dtype)
-
-    @pl.loop(1, regions)
-    def _(d):
-        to_region(home_out, home_in, home_send, home_recv, d).start()
+        if d > 0:
+            to_region(home_out, home_in, home_send, home_recv, d).start()
 
     @pl.loop(0, blocks)
     def _(b):

time: 84 us -> 84.1 us (level)
  no operation moved by 1% of the time
where the time goes in v6:
time: 84.1 us; the launch traced here: 83.9 us
  Pallas kernels  79.9 us (95%)
  other arithmetic  2.76 us (3%)
    pallas_call x1, Pallas kernels, per_device(): pl.pallas_call(functools.partial(kernel, regions, groups, levels), out_sh...  79.9 us
    div x1, other arithmetic, per_device(): return summed / (members * groups - 1)  1.89 us

profile of v6, /device:TPU:1, one launch (start us, length us, event | category | flops | bytes accessed | tf_op | source)
XLA Modules:
  0.0 83.9 jit_solution(1234713564422505446)
XLA Ops:
  0.7 0.7 fusion
  1.4 0.2 convert_reduce_fusion
  1.5 0.6 reshape.45.many_ref
  2.1 79.9 %shard_map.64 = f32[16,16,512]{2,1,0:T(8,128)} custom-call(s32[8]{0:T(128)} %bitcast.7, f32[64]{0:T(128)} %reshape.45.many_ref, bf16[16,256,512]{2,1,0:T(8,128)(2,1)} %bitcast.5, bf16[16,2,32,512]{3,2,1,0:T(8,128)(2,1)} %bitcast.6, bf16[16,2,512]{2,1,0:T(2,128)(2,1)} %where_ref.1), custom_call_target="tpu_custom_call" | custom-call | tf_op jit(solution)/shard_map/pallas_call | solution.py:328
  82.0 1.9 %broadcast_multiply_fusion = f32[16,16,512]{2,1,0:T(8,128)} fusion(f32[16,16,512]{2,1,0:T(8,128)} %shard_map.64), kind=kLoop, calls=%fused_computation | loop fusion | flops 131072 | bytes 1048576 | tf_op jit(solution)/shard_map/div | solution.py:365
  (2 shorter events, 0.0 us)

commit v7 on v6

--- a/solution.py
+++ b/solution.py
@@ -8,7 +8,7 @@
 from jax.sharding import PartitionSpec as P
 
 MESH = pl.DeviceIdType.MESH
-ROWS = 64
+ROWS = 128
 PIECE = (16, 256)
 TILE_BYTES = 24 << 20
 

time: 84.1 us -> 84.1 us (level)
  no operation moved by 1% of the time
where the time goes in v7:
time: 84.1 us; the launch traced here: 83.9 us
  Pallas kernels  79.9 us (95%)
  other arithmetic  2.76 us (3%)
    pallas_call x1, Pallas kernels, per_device(): pl.pallas_call(functools.partial(kernel, regions, groups, levels), out_sh...  79.9 us
    div x1, other arithmetic, per_device(): return summed / (members * groups - 1)  1.89 us

profile of v7, /device:TPU:1, one launch (start us, length us, event | category | flops | bytes accessed | tf_op | source)
XLA Modules:
  0.0 83.9 jit_solution(2195881664702711991)
XLA Ops:
  0.7 0.7 fusion
  1.4 0.2 convert_reduce_fusion
  1.5 0.6 reshape.45.many_ref
  2.1 79.9 %shard_map.64 = f32[16,16,512]{2,1,0:T(8,128)} custom-call(s32[8]{0:T(128)} %bitcast.7, f32[64]{0:T(128)} %reshape.45.many_ref, bf16[16,256,512]{2,1,0:T(8,128)(2,1)} %bitcast.5, bf16[16,2,32,512]{3,2,1,0:T(8,128)(2,1)} %bitcast.6, bf16[16,2,512]{2,1,0:T(2,128)(2,1)} %where_ref.1), custom_call_target="tpu_custom_call" | custom-call | tf_op jit(solution)/shard_map/pallas_call | solution.py:328
  82.0 1.9 %broadcast_multiply_fusion = f32[16,16,512]{2,1,0:T(8,128)} fusion(f32[16,16,512]{2,1,0:T(8,128)} %shard_map.64), kind=kLoop, calls=%fused_computation | loop fusion | flops 131072 | bytes 1048576 | tf_op jit(solution)/shard_map/div | solution.py:365
  (2 shorter events, 0.0 us)
